TPU v7x, 32 devices: a whole 2x2x4 slice. The times are simulated.
32 devices in a mesh: dp: 2 (over x), pipe: 2 (over core), ctx: 8 (over z, y).
Axes of the slice: x: 2, y: 2, z: 4, core: 2. Of those that a mesh axis runs over, the one named last changes fastest.
Arguments:
- section_input: bfloat16 [2, 2, 1024, 2048], P('dp', 'pipe', 'ctx'), may hold values from -6 to 6
- section_positions: int32 [2, 2, 1024], P('dp', 'pipe', 'ctx'), may hold values from 0 to 1023, as said below
- saved_input: bfloat16 [2, 2, 1024, 2048], P('dp', 'pipe', 'ctx'), may hold values from -6 to 6
- saved_positions: int32 [2, 2, 1024], P('dp', 'pipe', 'ctx'), may hold values from 0 to 1023, as said below
- cotangent: bfloat16 [2, 2, 1024, 2048], P('dp', 'pipe', 'ctx'), may hold values from -6 to 6
- norm_gains: float32 [2, 2, 2, 2048], P(None, 'pipe'), may hold values from -2 to 2
- output_gains: float32 [2, 2, 2048], P(None, 'pipe'), may hold values from 0.25 to 2
- plan: int32 [2, 2, 2], P('dp', 'pipe'), may hold values from 0 to 1
Outputs:
- next_input: bfloat16 [2, 2, 1024, 2048], P('dp', 'pipe', 'ctx')
- upstream_grad: bfloat16 [2, 2, 1024, 2048], P('dp', 'pipe', 'ctx')
- gain_grads: float32 [2, 3, 2048], P('pipe')
Inputs may be any that keep to these rules, and one draw needn't show every extreme that they name: `section_positions`: in every sequence the first position is 0 and each later one is either one more than the position before it or 0 (a new document). `saved_positions`: in every sequence the first position is 0 and each later one is either one more than the position before it or 0 (a new document).
All inputs are finite; a program needn't handle non-finite values.
Results may differ from a plain program's by a relative error of at most 0.0075.
Values may be sent and summed in bfloat16 or wider, within the bound.
A program may use at most 64 MiB of HBM per device.

v0:
```python
import jax
import jax.numpy as jnp
from jax import lax
from jax.sharding import PartitionSpec as P

HEADS = 16
HEAD_DIM = 128
FEATURES = 2048
WINDOW = 512
TOK_DEV = 128
EPSILON = 1e-06


def passed_along(value, axis, steps):
    count = lax.axis_size(axis)
    first, last = (max(0, -steps), min(count, count - steps))
    return lax.ppermute(value, axis, [(source, source + steps) for source in range(first, last)])


def shifted(value, axis, steps):
    count = lax.axis_size(axis)
    pairs = [(source, (source + steps) % count) for source in range(count)]
    return lax.ppermute(value, axis, pairs)


def as_bfloat(values):
    narrow = lax.optimization_barrier(values.astype(jnp.bfloat16)).astype(jnp.float32)
    return values + lax.stop_gradient(narrow - values)


def attend(key_rows, key_pos, key_ok, gains, query_count):
    total_rows = key_rows.shape[0]
    first_row = total_rows - query_count
    shaped = key_rows.reshape(total_rows, HEADS, HEAD_DIM)
    normed = shaped * lax.rsqrt(jnp.mean(shaped * shaped, axis=-1, keepdims=True) + EPSILON)
    query_gain = gains[0].reshape(HEADS, HEAD_DIM)
    key_gain = gains[1].reshape(HEADS, HEAD_DIM)
    queries = as_bfloat(normed[first_row:] * query_gain)
    key_vecs = as_bfloat(normed * key_gain)
    scores = jnp.einsum("qhe,khe->hqk", queries, key_vecs) / jnp.sqrt(jnp.float32(HEAD_DIM))
    query_ids = first_row + jnp.arange(query_count, dtype=jnp.int32)
    key_ids = jnp.arange(total_rows, dtype=jnp.int32)
    distance = query_ids[:, None] - key_ids[None, :]
    query_pos = key_pos[first_row:]
    allowed = (
        (distance >= 0)
        & (distance < WINDOW)
        & (query_pos[:, None] - key_pos[None, :] == distance)
        & key_ok[None, :]
    )
    weights = jnp.where(allowed[None], jnp.exp(scores), jnp.float32(0.0))
    probability = as_bfloat(weights / jnp.sum(weights, axis=-1, keepdims=True))
    mixture = jnp.einsum("hqk,khe->qhe", probability, shaped)
    return key_rows[first_row:] + mixture.reshape(query_count, FEATURES) * gains[2]


def pick_gains(norm_gains, output_gains, lap_index):
    pair_gains = lax.dynamic_index_in_dim(norm_gains, lap_index, 0, keepdims=False)[0]
    out_gain = lax.dynamic_index_in_dim(output_gains, lap_index, 0, keepdims=False)[0]
    return jnp.concatenate([pair_gains, out_gain[None]], axis=0)


def local(
    section_input,
    section_positions,
    saved_input,
    saved_positions,
    cotangent,
    norm_gains,
    output_gains,
    plan,
):
    own_rows = section_input[0, 0]
    own_pos = section_positions[0, 0]
    saved_rows = saved_input[0, 0]
    saved_pos = saved_positions[0, 0]
    incoming = cotangent[0, 0]
    shard_rows = own_rows.shape[0]
    piece_len = min(WINDOW, shard_rows)
    piece_count = WINDOW // piece_len
    shard_index = lax.axis_index("ctx")
    pieces = (own_rows, own_pos, saved_rows, saved_pos)
    received = []
    for reach in range(1, piece_count + 1):
        received.append(passed_along((pieces[0], pieces[1], pieces[2], pieces[3]), "ctx", reach))
    ordered = received[::-1]
    ok_parts = [
        jnp.broadcast_to(shard_index >= reach, (piece_len,)) for reach in range(piece_count, 0, -1)
    ]
    key_ok = jnp.concatenate(ok_parts + [jnp.ones((shard_rows,), bool)])
    forward_gains = pick_gains(norm_gains, output_gains, plan[0, 0, 0])
    backward_gains = pick_gains(norm_gains, output_gains, plan[0, 0, 1])
    forward_keys = jnp.concatenate([piece[0] for piece in ordered] + [own_rows], axis=0).astype(
        jnp.float32
    )
    forward_pos = jnp.concatenate([piece[1] for piece in ordered] + [own_pos], axis=0)
    produced = attend(forward_keys, forward_pos, key_ok, forward_gains, shard_rows).astype(
        jnp.bfloat16
    )
    next_input = shifted(produced, "pipe", 1)
    saved_keys = jnp.concatenate([piece[2] for piece in ordered] + [saved_rows], axis=0).astype(
        jnp.float32
    )
    saved_key_pos = jnp.concatenate([piece[3] for piece in ordered] + [saved_pos], axis=0)

    def local_layer(rows, gains):
        return attend(rows, saved_key_pos, key_ok, gains, shard_rows)

    _, pullback = jax.vjp(local_layer, saved_keys, backward_gains)
    key_grads, gain_grads = pullback(incoming.astype(jnp.float32))
    own_grads = key_grads[WINDOW:]
    arriving = jnp.zeros((piece_len, FEATURES), jnp.float32)
    for reach in range(1, piece_count + 1):
        first = (piece_count - reach) * piece_len
        outgoing = key_grads[first : first + piece_len].astype(jnp.bfloat16)
        arriving = arriving + passed_along(outgoing, "ctx", -reach).astype(jnp.float32)
    own_grads = own_grads.at[shard_rows - piece_len :].add(arriving)
    upstream_grad = shifted(own_grads.astype(jnp.bfloat16), "pipe", -1)
    gain_total = lax.psum(gain_grads, ("dp", "ctx"))
    gain_total = gain_total / jnp.float32(TOK_DEV)
    return (next_input[None, None], upstream_grad[None, None], gain_total[None])


def solution(mesh):
    placed = (
        P("dp", "pipe", "ctx", None),
        P("dp", "pipe", "ctx"),
        P("dp", "pipe", "ctx", None),
        P("dp", "pipe", "ctx"),
        P("dp", "pipe", "ctx", None),
        P(None, "pipe", None, None),
        P(None, "pipe", None),
        P("dp", "pipe", None),
    )
    return jax.shard_map(
        local,
        mesh=mesh,
        in_specs=placed,
        out_specs=(
            P("dp", "pipe", "ctx", None),
            P("dp", "pipe", "ctx", None),
            P("pipe", None, None),
        ),
        check_vma=False,
    )
```

profile of v0, /device:TPU:0, one launch (start us, length us, event | category | flops | bytes accessed | tf_op | source)
XLA Modules:
  0.0 320.6 jit_solution(6539457708362573059)
XLA Ops:
  0.6 6.0 %collective-permute-start.13 = (bf16[128,2048]{1,0:T(8,128)(2,1)}, bf16[128,2048]{1,0:T(8,128)(2,1)S(1)}, u32[]{:S(2)}, u32[]{:S(2)}) collective-permute-start(bf16[128,2048]{1,0:T(8,128)(2,1)} %bitcast.86), channel_id=1, source_target_pairs={{0,4},{1,5},{2,6},{3,7},{8,12},{9,13},{10,14},{11,15},{16,20},{17,... | collective-permute-start | bytes 1572872 | tf_op jit(solution)/shard_map/ppermute | solution.py:17
  6.6 4.5 %collective-permute-start.14 = (bf16[128,2048]{1,0:T(8,128)(2,1)}, bf16[128,2048]{1,0:T(8,128)(2,1)S(1)}, u32[]{:S(2)}, u32[]{:S(2)}) collective-permute-start(bf16[128,2048]{1,0:T(8,128)(2,1)} %bitcast.87), channel_id=1, source_target_pairs={{0,3},{1,4},{2,5},{3,6},{4,7},{8,11},{9,12},{10,13},{11,14},{12,15... | collective-permute-start | bytes 1572872 | tf_op jit(solution)/shard_map/ppermute | solution.py:17
  12.4 3.9 %collective-permute-start.16 = (bf16[128,2048]{1,0:T(8,128)(2,1)}, bf16[128,2048]{1,0:T(8,128)(2,1)}, u32[]{:S(2)}, u32[]{:S(2)}) collective-permute-start(bf16[128,2048]{1,0:T(8,128)(2,1)} %bitcast.89), channel_id=1, source_target_pairs={{0,1},{1,2},{2,3},{3,4},{4,5},{5,6},{6,7},{8,9},{9,10},{10,11},{11... | collective-permute-start | bytes 1572872 | tf_op jit(solution)/shard_map/ppermute | solution.py:17
  32.1 8.5 %collective-permute-done.4 = s32[128]{0:T(128)S(1)} collective-permute-done((s32[128]{0:T(128)}, s32[128]{0:T(128)S(1)}, u32[]{:S(2)}, u32[]{:S(2)}) %collective-permute-start.4) | collective-permute-done | bytes 544 | tf_op jit(solution)/shard_map/ppermute | solution.py:17
  40.6 38.0 %collective-permute-start.5 = (s32[128]{0:T(128)}, s32[128]{0:T(128)S(1)}, u32[]{:S(2)}, u32[]{:S(2)}) collective-permute-start(s32[128]{0:T(128)} %bitcast.117), channel_id=1, source_target_pairs={{0,3},{1,4},{2,5},{3,6},{4,7},{8,11},{9,12},{10,13},{11,14},{12,15... | collective-permute-start | bytes 1544 | tf_op jit(solution)/shard_map/ppermute | solution.py:17
  82.7 6.2 %collective-permute-start.7 = (s32[128]{0:T(128)}, s32[128]{0:T(128)S(1)}, u32[]{:S(2)}, u32[]{:S(2)}) collective-permute-start(s32[128]{0:T(128)} %bitcast.119), channel_id=1, source_target_pairs={{0,1},{1,2},{2,3},{3,4},{4,5},{5,6},{6,7},{8,9},{9,10},{10,11},{11... | collective-permute-start | bytes 1544 | tf_op jit(solution)/shard_map/ppermute | solution.py:17
  90.4 6.8 %collective-permute-start.9 = (s32[128]{0:T(128)}, s32[128]{0:T(128)S(1)}, u32[]{:S(2)}, u32[]{:S(2)}) collective-permute-start(s32[128]{0:T(128)} %bitcast.111), channel_id=1, source_target_pairs={{0,4},{1,5},{2,6},{3,7},{8,12},{9,13},{10,14},{11,15},{16,20},{17,... | collective-permute-start | bytes 1544 | tf_op jit(solution)/shard_map/ppermute | solution.py:17
  98.6 4.1 %collective-permute-start.10 = (s32[128]{0:T(128)}, s32[128]{0:T(128)S(1)}, u32[]{:S(2)}, u32[]{:S(2)}) collective-permute-start(s32[128]{0:T(128)} %bitcast.112), channel_id=1, source_target_pairs={{0,3},{1,4},{2,5},{3,6},{4,7},{8,11},{9,12},{10,13},{11,14},{12,15... | collective-permute-start | bytes 1544 | tf_op jit(solution)/shard_map/ppermute | solution.py:17
  104.2 3.4 %collective-permute-start.11 = (s32[128]{0:T(128)}, s32[128]{0:T(128)S(1)}, u32[]{:S(2)}, u32[]{:S(2)}) collective-permute-start(s32[128]{0:T(128)} %bitcast.113), channel_id=1, source_target_pairs={{0,2},{1,3},{2,4},{3,5},{4,6},{5,7},{8,10},{9,11},{10,12},{11,13},... | collective-permute-start | bytes 1544 | tf_op jit(solution)/shard_map/ppermute | solution.py:17
  109.0 4.1 %collective-permute-start.12 = (s32[128]{0:T(128)}, s32[128]{0:T(128)S(1)}, u32[]{:S(2)}, u32[]{:S(2)}) collective-permute-start(s32[128]{0:T(128)} %bitcast.114), channel_id=1, source_target_pairs={{0,1},{1,2},{2,3},{3,4},{4,5},{5,6},{6,7},{8,9},{9,10},{10,11},{11... | collective-permute-start | bytes 1544 | tf_op jit(solution)/shard_map/ppermute | solution.py:17
  114.5 19.6 %collective-permute-start = (bf16[128,2048]{1,0:T(8,128)(2,1)}, bf16[128,2048]{1,0:T(8,128)(2,1)}, u32[]{:S(2)}, u32[]{:S(2)}) collective-permute-start(bf16[128,2048]{1,0:T(8,128)(2,1)} %bitcast), channel_id=1, source_target_pairs={{0,4},{1,5},{2,6},{3,7},{8,12},{9,13},{10,14},{11,15},{16,20},{17,... | collective-permute-start | bytes 1572872 | tf_op jit(solution)/shard_map/ppermute | solution.py:17
  142.0 3.3 %collective-permute-start.3 = (bf16[128,2048]{1,0:T(8,128)(2,1)}, bf16[128,2048]{1,0:T(8,128)(2,1)}, u32[]{:S(2)}, u32[]{:S(2)}) collective-permute-start(bf16[128,2048]{1,0:T(8,128)(2,1)} %bitcast), channel_id=1, source_target_pairs={{0,1},{1,2},{2,3},{3,4},{4,5},{5,6},{6,7},{8,9},{9,10},{10,11},{11... | collective-permute-start | bytes 1572872 | tf_op jit(solution)/shard_map/ppermute | solution.py:17
  156.0 2.7 fusion.14
  158.8 4.1 %fusion.59 = (bf16[16,128,640]{2,1,0:T(8,128)(2,1)}, f32[16,128]{1,0:T(8,128)S(1)}, f32[16,128,640]{2,1,0:T(8,128)S(1)}) fusion(f32[16,128]{1,0:T(8,128)S(1)} %get-tuple-element.51, f32[16,128,640]{2,1,0:T(8,128)S(1)} %get-tuple-element.52, pred[128,640]{1,0:T(8,128)(4,1)S(1)} %get-tuple-element.45, f32[16,128]{1,0:T(8,128)S(1)} %multiply_divide_fusion, ...), kind=kOutput, calls=%fused_computation.121 | convolution fusion | flops 345241600 | bytes 16367616 | tf_op jit(solution)/shard_map/transpose(jvp(hqk,khe->qhe))/dot_general | solution.py:53
  162.9 3.4 %multiply_reduce_fusion.1 = (f32[16,128]{1,0:T(8,128)S(1)}, f32[128,16,128]{0,2,1:T(8,128)S(1)}) fusion(f32[640,16,128]{0,2,1:T(8,128)S(1)} %get-tuple-element.29, f32[16,128]{1,0:T(8,128)S(1)} %bitcast.104, bf16[640,16,128]{0,2,1:T(8,128)(2,1)S(1)} %get-tuple-element.30, bf16[640,16,128]{0,2,1:T(8,128)(2,1)S(1)} %constant_dynamic-update-slice_fusion.7, ...), kind=kOutput, calls=%fused_computation.58 | convolution fusion | flops 352057344 | bytes 17989632 | tf_op jit(solution)/shard_map/transpose(jvp(qhe,khe->hqk))/dot_general | solution.py:40
  166.3 3.9 %fusion.6 = (f32[16,128]{1,0:T(8,128)S(1)}, f32[640,16]{0,1:T(8,128)S(1)}, f32[16,640,128]{1,2,0:T(8,128)S(1)}) fusion(bf16[640,16,128]{0,2,1:T(8,128)(2,1)S(1)} %constant_dynamic-update-slice_fusion.7, f32[640,16]{0,1:T(8,128)S(1)} %fusion.54, f32[128,16,128]{0,2,1:T(8,128)S(1)} %get-tuple-element.38, f32[16,128]{1,0:T(8,128)S(1)} %bitcast.100, ...), kind=kOutput, calls=%fused_computation.19 | convolution fusion | flops 354930688 | bytes 21176320 | tf_op jit(solution)/shard_map/transpose(jvp(qhe,khe->hqk))/dot_general | solution.py:40
  170.3 4.0 %fusion.27 = f32[16,128]{1,0:T(8,128)S(1)} fusion(f32[128,16,128]{2,0,1:T(8,128)S(1)} %copy-done.2, bf16[640,16,128]{0,2,1:T(8,128)(2,1)S(1)} %constant_dynamic-update-slice_fusion.7, bf16[16,128,640]{2,1,0:T(8,128)(2,1)} %get-tuple-element.27, f32[16,128,640]{2,1,0:T(8,128)S(1)} %get-tuple-element.52, f32[16,128]{1,0:T(8,128)S(1)} %get-tuple-element.51, ...), kind=kOutput, calls=%fused_computation.50 | convolution fusion | flops 343930880 | bytes 11632640 | tf_op jit(solution)/shard_map/jvp(hqk,khe->qhe)/dot_general | solution.py:53
  174.3 4.9 %add_add_fusion = f32[640,16,128]{0,2,1:T(8,128)} fusion(bf16[640,16,128]{0,2,1:T(8,128)(2,1)S(1)} %constant_dynamic-update-slice_fusion.7, f32[128,16,128]{0,2,1:T(8,128)S(1)} %get-tuple-element.38, f32[16,640,128]{1,2,0:T(8,128)S(1)} %get-tuple-element.54, f32[640,16]{0,1:T(8,128)S(1)} %multiply_multiply_fusion.1, f32[16,128]{1,0:T(8,128)S(1)} %bitcast.101, ...), kind=kOutput, calls=%fused_computation.4 | convolution fusion | flops 354418688 | bytes 22732800 | tf_op jit(solution)/shard_map/transpose(jvp(hqk,khe->qhe))/dot_general | solution.py:53
  179.2 6.0 %copy.48 = f32[640,2048]{1,0:T(8,128)} copy(f32[640,2048]{0,1:T(8,128)} %bitcast.70) | data formatting | bytes 10485760 | tf_op jit(solution)/shard_map/transpose(jvp())/reshape | solution.py:34
  185.1 6.1 %fusion.60 = (bf16[640,2048]{1,0:T(8,128)(2,1)S(1)}, f32[640,2048]{1,0:T(8,128)}) fusion(f32[640,2048]{1,0:T(8,128)} %copy.48, bf16[128,2048]{1,0:T(8,128)(2,1)S(1)} %bitcast.84), kind=kLoop, calls=%fused_computation.122 | loop fusion | flops 3932160 | bytes 13631488 | tf_op jit(solution)/shard_map/convert.8
  212.9 2.8 fusion.12
  216.8 3.3 %fusion.2 = f32[16,128,128]{2,1,0:T(8,128)} fusion(bf16[640,16,128]{0,2,1:T(8,128)(2,1)S(1)} %constant_dynamic-update-slice_fusion, bf16[16,128,640]{2,1,0:T(8,128)(2,1)S(1)} %fusion.29, f32[16,128,640]{2,1,0:T(8,128)S(1)} %get-tuple-element.50, f32[16,128]{1,0:T(8,128)S(1)} %get-tuple-element.49, pred[128,640]{1,0:T(8,128)(4,1)S(1)} %get-tuple-element.46), kind=kOutput, calls=%fused_computation.13 | convolution fusion | flops 343408640 | bytes 11624448 | tf_op jit(solution)/shard_map/hqk,khe->qhe/dot_general | solution.py:53
  223.0 21.3 %collective-permute-done.20 = bf16[128,2048]{1,0:T(8,128)(2,1)} collective-permute-done((bf16[128,2048]{1,0:T(8,128)(2,1)}, bf16[128,2048]{1,0:T(8,128)(2,1)}, u32[]{:S(2)}, u32[]{:S(2)}) %collective-permute-start.20) | collective-permute-done | bytes 524320 | tf_op jit(solution)/shard_map/ppermute | solution.py:17
  246.6 71.7 %psum.7 = f32[3,2048]{1,0:T(4,128)S(1)} all-reduce(f32[3,2048]{1,0:T(4,128)S(1)} %pad_add_fusion), channel_id=1, replica_groups=mesh['dp'=2,'pipe'=2,'ctx'=8] {'dp','ctx'}, use_global_device_ids=true, to_apply=%region_9.10 | all-reduce | flops 6144 | bytes 49152 | tf_op jit(solution)/shard_map/psum | solution.py:119
  (110 shorter events, 72.8 us)
Async XLA Ops:
  0.6 135.2 %collective-permute-start.13 = (bf16[128,2048]{1,0:T(8,128)(2,1)}, bf16[128,2048]{1,0:T(8,128)(2,1)S(1)}, u32[]{:S(2)}, u32[]{:S(2)}) collective-permute-start(bf16[128,2048]{1,0:T(8,128)(2,1)} %bitcast.86), channel_id=1, source_target_pairs={{0,4},{1,5},{2,6},{3,7},{8,12},{9,13},{10,14},{11,15},{16,20},{17,... | collective-permute-start | bytes 1572872 | tf_op jit(solution)/shard_map/ppermute | solution.py:17
  6.6 132.3 %collective-permute-start.14 = (bf16[128,2048]{1,0:T(8,128)(2,1)}, bf16[128,2048]{1,0:T(8,128)(2,1)S(1)}, u32[]{:S(2)}, u32[]{:S(2)}) collective-permute-start(bf16[128,2048]{1,0:T(8,128)(2,1)} %bitcast.87), channel_id=1, source_target_pairs={{0,3},{1,4},{2,5},{3,6},{4,7},{8,11},{9,12},{10,13},{11,14},{12,15... | collective-permute-start | bytes 1572872 | tf_op jit(solution)/shard_map/ppermute | solution.py:17
  11.1 130.9 %collective-permute-start.15 = (bf16[128,2048]{1,0:T(8,128)(2,1)}, bf16[128,2048]{1,0:T(8,128)(2,1)S(1)}, u32[]{:S(2)}, u32[]{:S(2)}) collective-permute-start(bf16[128,2048]{1,0:T(8,128)(2,1)} %bitcast.88), channel_id=1, source_target_pairs={{0,2},{1,3},{2,4},{3,5},{4,6},{5,7},{8,10},{9,11},{10,12},{11,13},... | collective-permute-start | bytes 1572872 | tf_op jit(solution)/shard_map/ppermute | solution.py:17
  12.4 137.4 %collective-permute-start.16 = (bf16[128,2048]{1,0:T(8,128)(2,1)}, bf16[128,2048]{1,0:T(8,128)(2,1)}, u32[]{:S(2)}, u32[]{:S(2)}) collective-permute-start(bf16[128,2048]{1,0:T(8,128)(2,1)} %bitcast.89), channel_id=1, source_target_pairs={{0,1},{1,2},{2,3},{3,4},{4,5},{5,6},{6,7},{8,9},{9,10},{10,11},{11... | collective-permute-start | bytes 1572872 | tf_op jit(solution)/shard_map/ppermute | solution.py:17
  16.3 24.3 %collective-permute-start.4 = (s32[128]{0:T(128)}, s32[128]{0:T(128)S(1)}, u32[]{:S(2)}, u32[]{:S(2)}) collective-permute-start(s32[128]{0:T(128)} %bitcast.116), channel_id=1, source_target_pairs={{0,4},{1,5},{2,6},{3,7},{8,12},{9,13},{10,14},{11,15},{16,20},{17,... | collective-permute-start | bytes 1544 | tf_op jit(solution)/shard_map/ppermute | solution.py:17
  40.6 39.4 %collective-permute-start.5 = (s32[128]{0:T(128)}, s32[128]{0:T(128)S(1)}, u32[]{:S(2)}, u32[]{:S(2)}) collective-permute-start(s32[128]{0:T(128)} %bitcast.117), channel_id=1, source_target_pairs={{0,3},{1,4},{2,5},{3,6},{4,7},{8,11},{9,12},{10,13},{11,14},{12,15... | collective-permute-start | bytes 1544 | tf_op jit(solution)/shard_map/ppermute | solution.py:17
  80.0 2.7 collective-permute-start.6
  82.7 7.6 %collective-permute-start.7 = (s32[128]{0:T(128)}, s32[128]{0:T(128)S(1)}, u32[]{:S(2)}, u32[]{:S(2)}) collective-permute-start(s32[128]{0:T(128)} %bitcast.119), channel_id=1, source_target_pairs={{0,1},{1,2},{2,3},{3,4},{4,5},{5,6},{6,7},{8,9},{9,10},{10,11},{11... | collective-permute-start | bytes 1544 | tf_op jit(solution)/shard_map/ppermute | solution.py:17
  90.4 8.2 %collective-permute-start.9 = (s32[128]{0:T(128)}, s32[128]{0:T(128)S(1)}, u32[]{:S(2)}, u32[]{:S(2)}) collective-permute-start(s32[128]{0:T(128)} %bitcast.111), channel_id=1, source_target_pairs={{0,4},{1,5},{2,6},{3,7},{8,12},{9,13},{10,14},{11,15},{16,20},{17,... | collective-permute-start | bytes 1544 | tf_op jit(solution)/shard_map/ppermute | solution.py:17
  98.6 5.6 %collective-permute-start.10 = (s32[128]{0:T(128)}, s32[128]{0:T(128)S(1)}, u32[]{:S(2)}, u32[]{:S(2)}) collective-permute-start(s32[128]{0:T(128)} %bitcast.112), channel_id=1, source_target_pairs={{0,3},{1,4},{2,5},{3,6},{4,7},{8,11},{9,12},{10,13},{11,14},{12,15... | collective-permute-start | bytes 1544 | tf_op jit(solution)/shard_map/ppermute | solution.py:17
  104.2 4.8 %collective-permute-start.11 = (s32[128]{0:T(128)}, s32[128]{0:T(128)S(1)}, u32[]{:S(2)}, u32[]{:S(2)}) collective-permute-start(s32[128]{0:T(128)} %bitcast.113), channel_id=1, source_target_pairs={{0,2},{1,3},{2,4},{3,5},{4,6},{5,7},{8,10},{9,11},{10,12},{11,13},... | collective-permute-start | bytes 1544 | tf_op jit(solution)/shard_map/ppermute | solution.py:17
  109.0 5.6 %collective-permute-start.12 = (s32[128]{0:T(128)}, s32[128]{0:T(128)S(1)}, u32[]{:S(2)}, u32[]{:S(2)}) collective-permute-start(s32[128]{0:T(128)} %bitcast.114), channel_id=1, source_target_pairs={{0,1},{1,2},{2,3},{3,4},{4,5},{5,6},{6,7},{8,9},{9,10},{10,11},{11... | collective-permute-start | bytes 1544 | tf_op jit(solution)/shard_map/ppermute | solution.py:17
  114.5 79.5 %collective-permute-start = (bf16[128,2048]{1,0:T(8,128)(2,1)}, bf16[128,2048]{1,0:T(8,128)(2,1)}, u32[]{:S(2)}, u32[]{:S(2)}) collective-permute-start(bf16[128,2048]{1,0:T(8,128)(2,1)} %bitcast), channel_id=1, source_target_pairs={{0,4},{1,5},{2,6},{3,7},{8,12},{9,13},{10,14},{11,15},{16,20},{17,... | collective-permute-start | bytes 1572872 | tf_op jit(solution)/shard_map/ppermute | solution.py:17
  135.8 61.6 %collective-permute-start.1 = (bf16[128,2048]{1,0:T(8,128)(2,1)}, bf16[128,2048]{1,0:T(8,128)(2,1)}, u32[]{:S(2)}, u32[]{:S(2)}) collective-permute-start(bf16[128,2048]{1,0:T(8,128)(2,1)} %bitcast), channel_id=1, source_target_pairs={{0,3},{1,4},{2,5},{3,6},{4,7},{8,11},{9,12},{10,13},{11,14},{12,15... | collective-permute-start | bytes 1572872 | tf_op jit(solution)/shard_map/ppermute | solution.py:17
  138.9 62.1 %collective-permute-start.2 = (bf16[128,2048]{1,0:T(8,128)(2,1)}, bf16[128,2048]{1,0:T(8,128)(2,1)}, u32[]{:S(2)}, u32[]{:S(2)}) collective-permute-start(bf16[128,2048]{1,0:T(8,128)(2,1)} %bitcast), channel_id=1, source_target_pairs={{0,2},{1,3},{2,4},{3,5},{4,6},{5,7},{8,10},{9,11},{10,12},{11,13},... | collective-permute-start | bytes 1572872 | tf_op jit(solution)/shard_map/ppermute | solution.py:17
  142.0 65.8 %collective-permute-start.3 = (bf16[128,2048]{1,0:T(8,128)(2,1)}, bf16[128,2048]{1,0:T(8,128)(2,1)}, u32[]{:S(2)}, u32[]{:S(2)}) collective-permute-start(bf16[128,2048]{1,0:T(8,128)(2,1)} %bitcast), channel_id=1, source_target_pairs={{0,1},{1,2},{2,3},{3,4},{4,5},{5,6},{6,7},{8,9},{9,10},{10,11},{11... | collective-permute-start | bytes 1572872 | tf_op jit(solution)/shard_map/ppermute | solution.py:17
  179.2 6.0 %copy-start.1 = (bf16[1,1,128,2048]{3,2,1,0:T(8,128)(2,1)S(1)}, bf16[1,1,128,2048]{3,2,1,0:T(8,128)(2,1)}, u32[]{:S(2)}) copy-start(bf16[1,1,128,2048]{3,2,1,0:T(8,128)(2,1)} %param.16) | copy-start | bytes 1572868
  192.6 18.4 %copy-start = (bf16[1,1,128,2048]{2,3,1,0:T(8,128)(2,1)S(1)}, bf16[1,1,128,2048]{2,3,1,0:T(8,128)(2,1)}, u32[]{:S(2)}) copy-start(bf16[1,1,128,2048]{2,3,1,0:T(8,128)(2,1)} %copy.34) | copy-start | bytes 1572868
  192.6 30.3 %collective-permute-start.17 = (bf16[128,2048]{1,0:T(8,128)(2,1)}, bf16[128,2048]{1,0:T(8,128)(2,1)}, u32[]{:S(2)}, u32[]{:S(2)}) collective-permute-start(bf16[128,2048]{1,0:T(8,128)(2,1)} %get-tuple-element.33), channel_id=1, source_target_pairs={{1,0},{2,1},{3,2},{4,3},{5,4},{6,5},{7,6},{9,8},{10,9},{11,10},{12... | collective-permute-start | bytes 1572872 | tf_op jit(solution)/shard_map/ppermute | solution.py:17
  194.1 28.9 %collective-permute-start.18 = (bf16[128,2048]{1,0:T(8,128)(2,1)}, bf16[128,2048]{1,0:T(8,128)(2,1)}, u32[]{:S(2)}, u32[]{:S(2)}) collective-permute-start(bf16[128,2048]{1,0:T(8,128)(2,1)} %get-tuple-element.36), channel_id=1, source_target_pairs={{2,0},{3,1},{4,2},{5,3},{6,4},{7,5},{10,8},{11,9},{12,10},{13,11},... | collective-permute-start | bytes 1572872 | tf_op jit(solution)/shard_map/ppermute | solution.py:17
  197.4 25.6 %collective-permute-start.19 = (bf16[128,2048]{1,0:T(8,128)(2,1)}, bf16[128,2048]{1,0:T(8,128)(2,1)}, u32[]{:S(2)}, u32[]{:S(2)}) collective-permute-start(bf16[128,2048]{1,0:T(8,128)(2,1)} %get-tuple-element.35), channel_id=1, source_target_pairs={{3,0},{4,1},{5,2},{6,3},{7,4},{11,8},{12,9},{13,10},{14,11},{15,12... | collective-permute-start | bytes 1572872 | tf_op jit(solution)/shard_map/ppermute | solution.py:17
  201.0 43.3 %collective-permute-start.20 = (bf16[128,2048]{1,0:T(8,128)(2,1)}, bf16[128,2048]{1,0:T(8,128)(2,1)}, u32[]{:S(2)}, u32[]{:S(2)}) collective-permute-start(bf16[128,2048]{1,0:T(8,128)(2,1)} %get-tuple-element.34), channel_id=1, source_target_pairs={{4,0},{5,1},{6,2},{7,3},{12,8},{13,9},{14,10},{15,11},{20,16},{21,... | collective-permute-start | bytes 1572872 | tf_op jit(solution)/shard_map/ppermute | solution.py:17
  222.9 96.1 %collective-permute-start.8 = (bf16[128,2048]{1,0:T(8,128)(2,1)S(1)}, bf16[128,2048]{1,0:T(8,128)(2,1)S(1)}, u32[]{:S(2)}, u32[]{:S(2)}) collective-permute-start(bf16[128,2048]{1,0:T(8,128)(2,1)S(1)} %add_convert_fusion), channel_id=1, source_target_pairs={{0,8},{8,0},{1,9},{9,1},{2,10},{10,2},{3,11},{11,3},{4,12},{12,4},... | collective-permute-start | bytes 1572872 | tf_op jit(solution)/shard_map/ppermute | solution.py:23
  246.5 72.5 %collective-permute-start.21 = (bf16[128,2048]{1,0:T(8,128)(2,1)S(1)}, bf16[128,2048]{1,0:T(8,128)(2,1)S(1)}, u32[]{:S(2)}, u32[]{:S(2)}) collective-permute-start(bf16[128,2048]{1,0:T(8,128)(2,1)S(1)} %fusion.30), channel_id=1, source_target_pairs={{0,8},{8,0},{1,9},{9,1},{2,10},{10,2},{3,11},{11,3},{4,12},{12,4},... | collective-permute-start | bytes 1572872 | tf_op jit(solution)/shard_map/ppermute | solution.py:23
  (2 other events, 7.9 us)
where the time goes:
time: 322 us; the launch traced here: 321 us
  starting transfers between devices  114 us (35%)
  blocking collectives  71.7 us (22%)
  local copies, waits for them, and re-layouts  47 us (15%)
  waiting for transfers between devices  39 us (12%)
  matrix products  29.1 us (9%)
  other arithmetic  15.1 us (5%)
  between operations  5.06 us (2%)
    ppermute x20, starting transfers between devices, passed_along(): lax.ppermute(value, axis, [(source, source + steps) for source in range(f...  113 us
    psum x1, blocking collectives, local(): gain_total = lax.psum(gain_grads, ('dp', 'ctx'))  71.7 us
    ppermute x20, waiting for transfers between devices, passed_along(): lax.ppermute(value, axis, [(source, source + steps) for source in range(f...  39 us
    unnamed x33, local copies, waits for them, and re-layouts  17.3 us
    dot_general x4, matrix products, attend(): mixture = jnp.einsum('hqk,khe->qhe', probability, shaped)  16.3 us
    ppermute x8, local copies, waits for them, and re-layouts, passed_along(): lax.ppermute(value, axis, [(source, source + steps) for source in range(f...  13.2 us
    dot_general x4, matrix products, attend(): jnp.einsum('qhe,khe->hqk', queries, key_vecs)  12.8 us
  transfers between devices with their start and end apart: 22, of which 9 were waited for; matrix products, arithmetic and copies ran while one was open for 28% of the time, Pallas kernels for 0%

commit v1 on v0

--- a/solution.py
+++ b/solution.py
@@ -9,6 +9,10 @@
 WINDOW = 512
 TOK_DEV = 128
 EPSILON = 1e-06
+
+
+def advance_view(group_axis, mesh_ax, message):
+    return lax.psum(lax.psum(message, group_axis), mesh_ax)
 
 
 def passed_along(value, axis, steps):
@@ -116,7 +120,7 @@
         arriving = arriving + passed_along(outgoing, "ctx", -reach).astype(jnp.float32)
     own_grads = own_grads.at[shard_rows - piece_len :].add(arriving)
     upstream_grad = shifted(own_grads.astype(jnp.bfloat16), "pipe", -1)
-    gain_total = lax.psum(gain_grads, ("dp", "ctx"))
+    gain_total = advance_view("ctx", "dp", gain_grads)
     gain_total = gain_total / jnp.float32(TOK_DEV)
     return (next_input[None, None], upstream_grad[None, None], gain_total[None])
 

time: 322 us -> 292 us (0.907)
  blocking collectives: 71.7 us -> 41.4 us
    psum x1 -> x2, blocking collectives: 71.7 us -> 41.4 us  [advance_view(): return lax.psum(lax.psum(message, group_axis), mesh_ax)]
  transfers between devices with their start and end apart: 22 -> 22, of which waited for: 9 -> 9; matrix products, arithmetic and copies ran while one was open for 28% -> 31% of each run, Pallas kernels for 0% -> 0%
where the time goes in v1:
time: 292 us; the launch traced here: 290 us
  starting transfers between devices  114 us (39%)
  local copies, waits for them, and re-layouts  47.1 us (16%)
  blocking collectives  41.4 us (14%)
  waiting for transfers between devices  38.9 us (13%)
  matrix products  29.1 us (10%)
  other arithmetic  15.1 us (5%)
  between operations  5.07 us (2%)
    ppermute x20, starting transfers between devices, passed_along(): lax.ppermute(value, axis, [(source, source + steps) for source in range(f...  113 us
    psum x2, blocking collectives, advance_view(): return lax.psum(lax.psum(message, group_axis), mesh_ax)  41.4 us
    ppermute x20, waiting for transfers between devices, passed_along(): lax.ppermute(value, axis, [(source, source + steps) for source in range(f...  38.9 us
    unnamed x33, local copies, waits for them, and re-layouts  17.3 us
    dot_general x4, matrix products, attend(): mixture = jnp.einsum('hqk,khe->qhe', probability, shaped)  16.4 us
    ppermute x8, local copies, waits for them, and re-layouts, passed_along(): lax.ppermute(value, axis, [(source, source + steps) for source in range(f...  13.2 us
    dot_general x4, matrix products, attend(): jnp.einsum('qhe,khe->hqk', queries, key_vecs)  12.8 us
    another operation x1, other arithmetic  6.1 us
  transfers between devices with their start and end apart: 22, of which 9 were waited for; matrix products, arithmetic and copies ran while one was open for 31% of the time, Pallas kernels for 0%

profile of v1, /device:TPU:0, one launch (start us, length us, event | category | flops | bytes accessed | tf_op | source)
XLA Modules:
  0.0 290.2 jit_solution(6523721736747936232)
XLA Ops:
  0.6 6.0 %collective-permute-start.13 = (bf16[128,2048]{1,0:T(8,128)(2,1)}, bf16[128,2048]{1,0:T(8,128)(2,1)S(1)}, u32[]{:S(2)}, u32[]{:S(2)}) collective-permute-start(bf16[128,2048]{1,0:T(8,128)(2,1)} %bitcast.86), channel_id=1, source_target_pairs={{0,4},{1,5},{2,6},{3,7},{8,12},{9,13},{10,14},{11,15},{16,20},{17,... | collective-permute-start | bytes 1572872 | tf_op jit(solution)/shard_map/ppermute | solution.py:21
  6.6 4.5 %collective-permute-start.14 = (bf16[128,2048]{1,0:T(8,128)(2,1)}, bf16[128,2048]{1,0:T(8,128)(2,1)S(1)}, u32[]{:S(2)}, u32[]{:S(2)}) collective-permute-start(bf16[128,2048]{1,0:T(8,128)(2,1)} %bitcast.87), channel_id=1, source_target_pairs={{0,3},{1,4},{2,5},{3,6},{4,7},{8,11},{9,12},{10,13},{11,14},{12,15... | collective-permute-start | bytes 1572872 | tf_op jit(solution)/shard_map/ppermute | solution.py:21
  12.4 3.9 %collective-permute-start.16 = (bf16[128,2048]{1,0:T(8,128)(2,1)}, bf16[128,2048]{1,0:T(8,128)(2,1)}, u32[]{:S(2)}, u32[]{:S(2)}) collective-permute-start(bf16[128,2048]{1,0:T(8,128)(2,1)} %bitcast.89), channel_id=1, source_target_pairs={{0,1},{1,2},{2,3},{3,4},{4,5},{5,6},{6,7},{8,9},{9,10},{10,11},{11... | collective-permute-start | bytes 1572872 | tf_op jit(solution)/shard_map/ppermute | solution.py:21
  32.1 8.5 %collective-permute-done.4 = s32[128]{0:T(128)S(1)} collective-permute-done((s32[128]{0:T(128)}, s32[128]{0:T(128)S(1)}, u32[]{:S(2)}, u32[]{:S(2)}) %collective-permute-start.4) | collective-permute-done | bytes 544 | tf_op jit(solution)/shard_map/ppermute | solution.py:21
  40.6 38.0 %collective-permute-start.5 = (s32[128]{0:T(128)}, s32[128]{0:T(128)S(1)}, u32[]{:S(2)}, u32[]{:S(2)}) collective-permute-start(s32[128]{0:T(128)} %bitcast.117), channel_id=1, source_target_pairs={{0,3},{1,4},{2,5},{3,6},{4,7},{8,11},{9,12},{10,13},{11,14},{12,15... | collective-permute-start | bytes 1544 | tf_op jit(solution)/shard_map/ppermute | solution.py:21
  82.7 6.2 %collective-permute-start.7 = (s32[128]{0:T(128)}, s32[128]{0:T(128)S(1)}, u32[]{:S(2)}, u32[]{:S(2)}) collective-permute-start(s32[128]{0:T(128)} %bitcast.119), channel_id=1, source_target_pairs={{0,1},{1,2},{2,3},{3,4},{4,5},{5,6},{6,7},{8,9},{9,10},{10,11},{11... | collective-permute-start | bytes 1544 | tf_op jit(solution)/shard_map/ppermute | solution.py:21
  90.4 6.8 %collective-permute-start.9 = (s32[128]{0:T(128)}, s32[128]{0:T(128)S(1)}, u32[]{:S(2)}, u32[]{:S(2)}) collective-permute-start(s32[128]{0:T(128)} %bitcast.111), channel_id=1, source_target_pairs={{0,4},{1,5},{2,6},{3,7},{8,12},{9,13},{10,14},{11,15},{16,20},{17,... | collective-permute-start | bytes 1544 | tf_op jit(solution)/shard_map/ppermute | solution.py:21
  98.6 4.1 %collective-permute-start.10 = (s32[128]{0:T(128)}, s32[128]{0:T(128)S(1)}, u32[]{:S(2)}, u32[]{:S(2)}) collective-permute-start(s32[128]{0:T(128)} %bitcast.112), channel_id=1, source_target_pairs={{0,3},{1,4},{2,5},{3,6},{4,7},{8,11},{9,12},{10,13},{11,14},{12,15... | collective-permute-start | bytes 1544 | tf_op jit(solution)/shard_map/ppermute | solution.py:21
  104.2 3.4 %collective-permute-start.11 = (s32[128]{0:T(128)}, s32[128]{0:T(128)S(1)}, u32[]{:S(2)}, u32[]{:S(2)}) collective-permute-start(s32[128]{0:T(128)} %bitcast.113), channel_id=1, source_target_pairs={{0,2},{1,3},{2,4},{3,5},{4,6},{5,7},{8,10},{9,11},{10,12},{11,13},... | collective-permute-start | bytes 1544 | tf_op jit(solution)/shard_map/ppermute | solution.py:21
  109.0 4.1 %collective-permute-start.12 = (s32[128]{0:T(128)}, s32[128]{0:T(128)S(1)}, u32[]{:S(2)}, u32[]{:S(2)}) collective-permute-start(s32[128]{0:T(128)} %bitcast.114), channel_id=1, source_target_pairs={{0,1},{1,2},{2,3},{3,4},{4,5},{5,6},{6,7},{8,9},{9,10},{10,11},{11... | collective-permute-start | bytes 1544 | tf_op jit(solution)/shard_map/ppermute | solution.py:21
  114.5 19.6 %collective-permute-start = (bf16[128,2048]{1,0:T(8,128)(2,1)}, bf16[128,2048]{1,0:T(8,128)(2,1)}, u32[]{:S(2)}, u32[]{:S(2)}) collective-permute-start(bf16[128,2048]{1,0:T(8,128)(2,1)} %bitcast), channel_id=1, source_target_pairs={{0,4},{1,5},{2,6},{3,7},{8,12},{9,13},{10,14},{11,15},{16,20},{17,... | collective-permute-start | bytes 1572872 | tf_op jit(solution)/shard_map/ppermute | solution.py:21
  142.0 3.4 %collective-permute-start.3 = (bf16[128,2048]{1,0:T(8,128)(2,1)}, bf16[128,2048]{1,0:T(8,128)(2,1)}, u32[]{:S(2)}, u32[]{:S(2)}) collective-permute-start(bf16[128,2048]{1,0:T(8,128)(2,1)} %bitcast), channel_id=1, source_target_pairs={{0,1},{1,2},{2,3},{3,4},{4,5},{5,6},{6,7},{8,9},{9,10},{10,11},{11... | collective-permute-start | bytes 1572872 | tf_op jit(solution)/shard_map/ppermute | solution.py:21
  158.8 4.1 %fusion.59 = (bf16[16,128,640]{2,1,0:T(8,128)(2,1)}, f32[16,128]{1,0:T(8,128)S(1)}, f32[16,128,640]{2,1,0:T(8,128)S(1)}) fusion(f32[16,128]{1,0:T(8,128)S(1)} %get-tuple-element.51, f32[16,128,640]{2,1,0:T(8,128)S(1)} %get-tuple-element.52, pred[128,640]{1,0:T(8,128)(4,1)S(1)} %get-tuple-element.45, f32[16,128]{1,0:T(8,128)S(1)} %multiply_divide_fusion, ...), kind=kOutput, calls=%fused_computation.121 | convolution fusion | flops 345241600 | bytes 16367616 | tf_op jit(solution)/shard_map/transpose(jvp(hqk,khe->qhe))/dot_general | solution.py:57
  162.9 3.4 %multiply_reduce_fusion.1 = (f32[16,128]{1,0:T(8,128)S(1)}, f32[128,16,128]{0,2,1:T(8,128)S(1)}) fusion(f32[640,16,128]{0,2,1:T(8,128)S(1)} %get-tuple-element.29, f32[16,128]{1,0:T(8,128)S(1)} %bitcast.104, bf16[640,16,128]{0,2,1:T(8,128)(2,1)S(1)} %get-tuple-element.30, bf16[640,16,128]{0,2,1:T(8,128)(2,1)S(1)} %constant_dynamic-update-slice_fusion.7, ...), kind=kOutput, calls=%fused_computation.58 | convolution fusion | flops 352057344 | bytes 17989632 | tf_op jit(solution)/shard_map/transpose(jvp(qhe,khe->hqk))/dot_general | solution.py:44
  166.3 3.9 %fusion.6 = (f32[16,128]{1,0:T(8,128)S(1)}, f32[640,16]{0,1:T(8,128)S(1)}, f32[16,640,128]{1,2,0:T(8,128)S(1)}) fusion(bf16[640,16,128]{0,2,1:T(8,128)(2,1)S(1)} %constant_dynamic-update-slice_fusion.7, f32[640,16]{0,1:T(8,128)S(1)} %fusion.54, f32[128,16,128]{0,2,1:T(8,128)S(1)} %get-tuple-element.38, f32[16,128]{1,0:T(8,128)S(1)} %bitcast.100, ...), kind=kOutput, calls=%fused_computation.19 | convolution fusion | flops 354930688 | bytes 21176320 | tf_op jit(solution)/shard_map/transpose(jvp(qhe,khe->hqk))/dot_general | solution.py:44
  170.3 4.0 %fusion.27 = f32[16,128]{1,0:T(8,128)S(1)} fusion(f32[128,16,128]{2,0,1:T(8,128)S(1)} %copy-done.2, bf16[640,16,128]{0,2,1:T(8,128)(2,1)S(1)} %constant_dynamic-update-slice_fusion.7, bf16[16,128,640]{2,1,0:T(8,128)(2,1)} %get-tuple-element.27, f32[16,128,640]{2,1,0:T(8,128)S(1)} %get-tuple-element.52, f32[16,128]{1,0:T(8,128)S(1)} %get-tuple-element.51, ...), kind=kOutput, calls=%fused_computation.50 | convolution fusion | flops 343930880 | bytes 11632640 | tf_op jit(solution)/shard_map/jvp(hqk,khe->qhe)/dot_general | solution.py:57
  174.3 4.9 %add_add_fusion = f32[640,16,128]{0,2,1:T(8,128)} fusion(bf16[640,16,128]{0,2,1:T(8,128)(2,1)S(1)} %constant_dynamic-update-slice_fusion.7, f32[128,16,128]{0,2,1:T(8,128)S(1)} %get-tuple-element.38, f32[16,640,128]{1,2,0:T(8,128)S(1)} %get-tuple-element.54, f32[640,16]{0,1:T(8,128)S(1)} %multiply_multiply_fusion.1, f32[16,128]{1,0:T(8,128)S(1)} %bitcast.101, ...), kind=kOutput, calls=%fused_computation.4 | convolution fusion | flops 354418688 | bytes 22732800 | tf_op jit(solution)/shard_map/transpose(jvp(hqk,khe->qhe))/dot_general | solution.py:57
  179.2 6.1 %copy.48 = f32[640,2048]{1,0:T(8,128)} copy(f32[640,2048]{0,1:T(8,128)} %bitcast.70) | data formatting | bytes 10485760 | tf_op jit(solution)/shard_map/transpose(jvp())/reshape | solution.py:38
  185.2 6.1 %fusion.60 = (bf16[640,2048]{1,0:T(8,128)(2,1)S(1)}, f32[640,2048]{1,0:T(8,128)}) fusion(f32[640,2048]{1,0:T(8,128)} %copy.48, bf16[128,2048]{1,0:T(8,128)(2,1)S(1)} %bitcast.84), kind=kLoop, calls=%fused_computation.122 | loop fusion | flops 3932160 | bytes 13631488 | tf_op jit(solution)/shard_map/convert.8
  213.0 2.8 fusion.12
  216.9 3.4 %fusion.2 = f32[16,128,128]{2,1,0:T(8,128)} fusion(bf16[640,16,128]{0,2,1:T(8,128)(2,1)S(1)} %constant_dynamic-update-slice_fusion, bf16[16,128,640]{2,1,0:T(8,128)(2,1)S(1)} %fusion.29, f32[16,128,640]{2,1,0:T(8,128)S(1)} %get-tuple-element.50, f32[16,128]{1,0:T(8,128)S(1)} %get-tuple-element.49, pred[128,640]{1,0:T(8,128)(4,1)S(1)} %get-tuple-element.46), kind=kOutput, calls=%fused_computation.13 | convolution fusion | flops 343408640 | bytes 11624448 | tf_op jit(solution)/shard_map/hqk,khe->qhe/dot_general | solution.py:57
  223.1 21.2 %collective-permute-done.20 = bf16[128,2048]{1,0:T(8,128)(2,1)} collective-permute-done((bf16[128,2048]{1,0:T(8,128)(2,1)}, bf16[128,2048]{1,0:T(8,128)(2,1)}, u32[]{:S(2)}, u32[]{:S(2)}) %collective-permute-start.20) | collective-permute-done | bytes 524320 | tf_op jit(solution)/shard_map/ppermute | solution.py:21
  246.7 33.0 %psum.14 = f32[3,2048]{1,0:T(4,128)S(1)} all-reduce(f32[3,2048]{1,0:T(4,128)S(1)} %pad_add_fusion), channel_id=1, replica_groups=mesh['dp'=2,'pipe'=2,'ctx'=8] {'ctx'}, use_global_device_ids=true, to_apply=%region_9.10 | all-reduce | flops 6144 | bytes 49152 | tf_op jit(solution)/shard_map/psum | solution.py:15
  279.7 8.3 %psum.15 = f32[3,2048]{1,0:T(4,128)S(1)} all-reduce(f32[3,2048]{1,0:T(4,128)S(1)} %psum.14), channel_id=1, replica_groups=mesh['dp'=2,'pipe'=2,'ctx'=8] {'dp'}, use_global_device_ids=true, to_apply=%region_10.11 | all-reduce | flops 6144 | bytes 49152 | tf_op jit(solution)/shard_map/psum | solution.py:15
  (111 shorter events, 75.6 us)
Async XLA Ops:
  0.6 135.2 %collective-permute-start.13 = (bf16[128,2048]{1,0:T(8,128)(2,1)}, bf16[128,2048]{1,0:T(8,128)(2,1)S(1)}, u32[]{:S(2)}, u32[]{:S(2)}) collective-permute-start(bf16[128,2048]{1,0:T(8,128)(2,1)} %bitcast.86), channel_id=1, source_target_pairs={{0,4},{1,5},{2,6},{3,7},{8,12},{9,13},{10,14},{11,15},{16,20},{17,... | collective-permute-start | bytes 1572872 | tf_op jit(solution)/shard_map/ppermute | solution.py:21
  6.6 132.3 %collective-permute-start.14 = (bf16[128,2048]{1,0:T(8,128)(2,1)}, bf16[128,2048]{1,0:T(8,128)(2,1)S(1)}, u32[]{:S(2)}, u32[]{:S(2)}) collective-permute-start(bf16[128,2048]{1,0:T(8,128)(2,1)} %bitcast.87), channel_id=1, source_target_pairs={{0,3},{1,4},{2,5},{3,6},{4,7},{8,11},{9,12},{10,13},{11,14},{12,15... | collective-permute-start | bytes 1572872 | tf_op jit(solution)/shard_map/ppermute | solution.py:21
  11.1 130.9 %collective-permute-start.15 = (bf16[128,2048]{1,0:T(8,128)(2,1)}, bf16[128,2048]{1,0:T(8,128)(2,1)S(1)}, u32[]{:S(2)}, u32[]{:S(2)}) collective-permute-start(bf16[128,2048]{1,0:T(8,128)(2,1)} %bitcast.88), channel_id=1, source_target_pairs={{0,2},{1,3},{2,4},{3,5},{4,6},{5,7},{8,10},{9,11},{10,12},{11,13},... | collective-permute-start | bytes 1572872 | tf_op jit(solution)/shard_map/ppermute | solution.py:21
  12.4 137.4 %collective-permute-start.16 = (bf16[128,2048]{1,0:T(8,128)(2,1)}, bf16[128,2048]{1,0:T(8,128)(2,1)}, u32[]{:S(2)}, u32[]{:S(2)}) collective-permute-start(bf16[128,2048]{1,0:T(8,128)(2,1)} %bitcast.89), channel_id=1, source_target_pairs={{0,1},{1,2},{2,3},{3,4},{4,5},{5,6},{6,7},{8,9},{9,10},{10,11},{11... | collective-permute-start | bytes 1572872 | tf_op jit(solution)/shard_map/ppermute | solution.py:21
  16.3 24.3 %collective-permute-start.4 = (s32[128]{0:T(128)}, s32[128]{0:T(128)S(1)}, u32[]{:S(2)}, u32[]{:S(2)}) collective-permute-start(s32[128]{0:T(128)} %bitcast.116), channel_id=1, source_target_pairs={{0,4},{1,5},{2,6},{3,7},{8,12},{9,13},{10,14},{11,15},{16,20},{17,... | collective-permute-start | bytes 1544 | tf_op jit(solution)/shard_map/ppermute | solution.py:21
  40.6 39.4 %collective-permute-start.5 = (s32[128]{0:T(128)}, s32[128]{0:T(128)S(1)}, u32[]{:S(2)}, u32[]{:S(2)}) collective-permute-start(s32[128]{0:T(128)} %bitcast.117), channel_id=1, source_target_pairs={{0,3},{1,4},{2,5},{3,6},{4,7},{8,11},{9,12},{10,13},{11,14},{12,15... | collective-permute-start | bytes 1544 | tf_op jit(solution)/shard_map/ppermute | solution.py:21
  80.0 2.7 collective-permute-start.6
  82.7 7.6 %collective-permute-start.7 = (s32[128]{0:T(128)}, s32[128]{0:T(128)S(1)}, u32[]{:S(2)}, u32[]{:S(2)}) collective-permute-start(s32[128]{0:T(128)} %bitcast.119), channel_id=1, source_target_pairs={{0,1},{1,2},{2,3},{3,4},{4,5},{5,6},{6,7},{8,9},{9,10},{10,11},{11... | collective-permute-start | bytes 1544 | tf_op jit(solution)/shard_map/ppermute | solution.py:21
  90.4 8.2 %collective-permute-start.9 = (s32[128]{0:T(128)}, s32[128]{0:T(128)S(1)}, u32[]{:S(2)}, u32[]{:S(2)}) collective-permute-start(s32[128]{0:T(128)} %bitcast.111), channel_id=1, source_target_pairs={{0,4},{1,5},{2,6},{3,7},{8,12},{9,13},{10,14},{11,15},{16,20},{17,... | collective-permute-start | bytes 1544 | tf_op jit(solution)/shard_map/ppermute | solution.py:21
  98.6 5.6 %collective-permute-start.10 = (s32[128]{0:T(128)}, s32[128]{0:T(128)S(1)}, u32[]{:S(2)}, u32[]{:S(2)}) collective-permute-start(s32[128]{0:T(128)} %bitcast.112), channel_id=1, source_target_pairs={{0,3},{1,4},{2,5},{3,6},{4,7},{8,11},{9,12},{10,13},{11,14},{12,15... | collective-permute-start | bytes 1544 | tf_op jit(solution)/shard_map/ppermute | solution.py:21
  104.2 4.8 %collective-permute-start.11 = (s32[128]{0:T(128)}, s32[128]{0:T(128)S(1)}, u32[]{:S(2)}, u32[]{:S(2)}) collective-permute-start(s32[128]{0:T(128)} %bitcast.113), channel_id=1, source_target_pairs={{0,2},{1,3},{2,4},{3,5},{4,6},{5,7},{8,10},{9,11},{10,12},{11,13},... | collective-permute-start | bytes 1544 | tf_op jit(solution)/shard_map/ppermute | solution.py:21
  109.0 5.6 %collective-permute-start.12 = (s32[128]{0:T(128)}, s32[128]{0:T(128)S(1)}, u32[]{:S(2)}, u32[]{:S(2)}) collective-permute-start(s32[128]{0:T(128)} %bitcast.114), channel_id=1, source_target_pairs={{0,1},{1,2},{2,3},{3,4},{4,5},{5,6},{6,7},{8,9},{9,10},{10,11},{11... | collective-permute-start | bytes 1544 | tf_op jit(solution)/shard_map/ppermute | solution.py:21
  114.5 79.6 %collective-permute-start = (bf16[128,2048]{1,0:T(8,128)(2,1)}, bf16[128,2048]{1,0:T(8,128)(2,1)}, u32[]{:S(2)}, u32[]{:S(2)}) collective-permute-start(bf16[128,2048]{1,0:T(8,128)(2,1)} %bitcast), channel_id=1, source_target_pairs={{0,4},{1,5},{2,6},{3,7},{8,12},{9,13},{10,14},{11,15},{16,20},{17,... | collective-permute-start | bytes 1572872 | tf_op jit(solution)/shard_map/ppermute | solution.py:21
  135.8 61.7 %collective-permute-start.1 = (bf16[128,2048]{1,0:T(8,128)(2,1)}, bf16[128,2048]{1,0:T(8,128)(2,1)}, u32[]{:S(2)}, u32[]{:S(2)}) collective-permute-start(bf16[128,2048]{1,0:T(8,128)(2,1)} %bitcast), channel_id=1, source_target_pairs={{0,3},{1,4},{2,5},{3,6},{4,7},{8,11},{9,12},{10,13},{11,14},{12,15... | collective-permute-start | bytes 1572872 | tf_op jit(solution)/shard_map/ppermute | solution.py:21
  138.9 62.1 %collective-permute-start.2 = (bf16[128,2048]{1,0:T(8,128)(2,1)}, bf16[128,2048]{1,0:T(8,128)(2,1)}, u32[]{:S(2)}, u32[]{:S(2)}) collective-permute-start(bf16[128,2048]{1,0:T(8,128)(2,1)} %bitcast), channel_id=1, source_target_pairs={{0,2},{1,3},{2,4},{3,5},{4,6},{5,7},{8,10},{9,11},{10,12},{11,13},... | collective-permute-start | bytes 1572872 | tf_op jit(solution)/shard_map/ppermute | solution.py:21
  142.0 65.9 %collective-permute-start.3 = (bf16[128,2048]{1,0:T(8,128)(2,1)}, bf16[128,2048]{1,0:T(8,128)(2,1)}, u32[]{:S(2)}, u32[]{:S(2)}) collective-permute-start(bf16[128,2048]{1,0:T(8,128)(2,1)} %bitcast), channel_id=1, source_target_pairs={{0,1},{1,2},{2,3},{3,4},{4,5},{5,6},{6,7},{8,9},{9,10},{10,11},{11... | collective-permute-start | bytes 1572872 | tf_op jit(solution)/shard_map/ppermute | solution.py:21
  179.2 6.1 %copy-start.1 = (bf16[1,1,128,2048]{3,2,1,0:T(8,128)(2,1)S(1)}, bf16[1,1,128,2048]{3,2,1,0:T(8,128)(2,1)}, u32[]{:S(2)}) copy-start(bf16[1,1,128,2048]{3,2,1,0:T(8,128)(2,1)} %param.16) | copy-start | bytes 1572868
  192.7 18.4 %copy-start = (bf16[1,1,128,2048]{2,3,1,0:T(8,128)(2,1)S(1)}, bf16[1,1,128,2048]{2,3,1,0:T(8,128)(2,1)}, u32[]{:S(2)}) copy-start(bf16[1,1,128,2048]{2,3,1,0:T(8,128)(2,1)} %copy.34) | copy-start | bytes 1572868
  192.7 30.3 %collective-permute-start.17 = (bf16[128,2048]{1,0:T(8,128)(2,1)}, bf16[128,2048]{1,0:T(8,128)(2,1)}, u32[]{:S(2)}, u32[]{:S(2)}) collective-permute-start(bf16[128,2048]{1,0:T(8,128)(2,1)} %get-tuple-element.33), channel_id=1, source_target_pairs={{1,0},{2,1},{3,2},{4,3},{5,4},{6,5},{7,6},{9,8},{10,9},{11,10},{12... | collective-permute-start | bytes 1572872 | tf_op jit(solution)/shard_map/ppermute | solution.py:21
  194.2 28.9 %collective-permute-start.18 = (bf16[128,2048]{1,0:T(8,128)(2,1)}, bf16[128,2048]{1,0:T(8,128)(2,1)}, u32[]{:S(2)}, u32[]{:S(2)}) collective-permute-start(bf16[128,2048]{1,0:T(8,128)(2,1)} %get-tuple-element.36), channel_id=1, source_target_pairs={{2,0},{3,1},{4,2},{5,3},{6,4},{7,5},{10,8},{11,9},{12,10},{13,11},... | collective-permute-start | bytes 1572872 | tf_op jit(solution)/shard_map/ppermute | solution.py:21
  197.5 25.6 %collective-permute-start.19 = (bf16[128,2048]{1,0:T(8,128)(2,1)}, bf16[128,2048]{1,0:T(8,128)(2,1)}, u32[]{:S(2)}, u32[]{:S(2)}) collective-permute-start(bf16[128,2048]{1,0:T(8,128)(2,1)} %get-tuple-element.35), channel_id=1, source_target_pairs={{3,0},{4,1},{5,2},{6,3},{7,4},{11,8},{12,9},{13,10},{14,11},{15,12... | collective-permute-start | bytes 1572872 | tf_op jit(solution)/shard_map/ppermute | solution.py:21
  201.1 43.3 %collective-permute-start.20 = (bf16[128,2048]{1,0:T(8,128)(2,1)}, bf16[128,2048]{1,0:T(8,128)(2,1)}, u32[]{:S(2)}, u32[]{:S(2)}) collective-permute-start(bf16[128,2048]{1,0:T(8,128)(2,1)} %get-tuple-element.34), channel_id=1, source_target_pairs={{4,0},{5,1},{6,2},{7,3},{12,8},{13,9},{14,10},{15,11},{20,16},{21,... | collective-permute-start | bytes 1572872 | tf_op jit(solution)/shard_map/ppermute | solution.py:21
  223.0 65.7 %collective-permute-start.8 = (bf16[128,2048]{1,0:T(8,128)(2,1)S(1)}, bf16[128,2048]{1,0:T(8,128)(2,1)S(1)}, u32[]{:S(2)}, u32[]{:S(2)}) collective-permute-start(bf16[128,2048]{1,0:T(8,128)(2,1)S(1)} %add_convert_fusion), channel_id=1, source_target_pairs={{0,8},{8,0},{1,9},{9,1},{2,10},{10,2},{3,11},{11,3},{4,12},{12,4},... | collective-permute-start | bytes 1572872 | tf_op jit(solution)/shard_map/ppermute | solution.py:27
  246.5 42.1 %collective-permute-start.21 = (bf16[128,2048]{1,0:T(8,128)(2,1)S(1)}, bf16[128,2048]{1,0:T(8,128)(2,1)S(1)}, u32[]{:S(2)}, u32[]{:S(2)}) collective-permute-start(bf16[128,2048]{1,0:T(8,128)(2,1)S(1)} %fusion.30), channel_id=1, source_target_pairs={{0,8},{8,0},{1,9},{9,1},{2,10},{10,2},{3,11},{11,3},{4,12},{12,4},... | collective-permute-start | bytes 1572872 | tf_op jit(solution)/shard_map/ppermute | solution.py:27
  (2 other events, 7.9 us)
